TPU v7x, 32 devices: a whole 2x2x4 slice. The times are simulated.
32 devices in a mesh: panel: 8 (over z, y), chan: 4 (over x, core).
Axes of the slice: x: 2, y: 2, z: 4, core: 2. Of those that a mesh axis runs over, the one named last changes fastest.
Arguments:
- wavefunction: bfloat16 [4, 8, 768, 768], P('chan', 'panel'), may hold values from -6 to 6
- left_env: bfloat16 [2, 8, 768, 768], P(None, 'panel'), may hold values from -0.21875 to 0.21875
- right_env: bfloat16 [2, 8, 768, 768], P(None, 'panel'), may hold values from -0.21875 to 0.21875
- coupling: float32 [2, 4, 4], replicated, may hold values from -4 to 4
- sec_size: int32 [8], replicated, may hold values from 384 to 768, as said below
Outputs:
- applied: bfloat16 [4, 8, 768, 768], P('chan', 'panel')
Inputs may be any that keep to these rules, and one draw needn't show every extreme that they name: `sec_size`: sector sizes; some sector holds exactly 768 states.
All inputs are finite; a program needn't handle non-finite values.
Results may differ from a plain program's by a relative error of at most 0.008.
Values may be sent and summed in bfloat16 or wider, within the bound.
A program may use at most 128 MiB of HBM per device.

v0:
```python
import jax
import jax.numpy as jnp
from jax import lax
from jax.sharding import PartitionSpec as P

CHARGE_TABLE = (0, 1, 1, 2)


def from_behind(block, axis, distance):
    devices = range(lax.axis_size(axis))
    route = [(i - distance, i) for i in devices if i - distance in devices]
    return lax.ppermute(block, axis, route)


def pick_entry(lookup_table, position):
    slot_ids = jnp.arange(lookup_table.shape[0], dtype=jnp.int32)
    return jnp.sum(jnp.where(slot_ids == position, lookup_table, jnp.zeros_like(lookup_table)))


def pick_column(matrix, position):
    slot_ids = jnp.arange(matrix.shape[1], dtype=jnp.int32)
    return jnp.sum(jnp.where(slot_ids[None, :] == position, matrix, 0.0), axis=1)


def outer_dot(left_matrix, right_matrix):
    return lax.dot_general(
        left_matrix, right_matrix, (((1,), (1,)), ((), ())), preferred_element_type=jnp.float32
    )


def coupling_masks(coupling):
    charges = jnp.array(CHARGE_TABLE, jnp.int32)
    same_charge = charges[:, None] == charges[None, :]
    raised_charge = charges[None, :] == charges[:, None] + 1
    return (jnp.where(same_charge, coupling[0], 0.0), jnp.where(raised_charge, coupling[1], 0.0))


def block_mask(sec_size, sector, charge, sector_width):
    sector_count = sec_size.shape[0]
    target = sector + charge
    exists = target < sector_count
    rows_live = pick_entry(sec_size, sector)
    cols_live = pick_entry(sec_size, target)
    positions = jnp.arange(sector_width, dtype=jnp.int32)
    row_ok = positions[:, None] < rows_live
    col_ok = positions[None, :] < cols_live
    return jnp.logical_and(jnp.logical_and(row_ok, col_ok), exists)


def choose_block(charge, own_block, near_block, far_block):
    return jnp.where(charge == 0, own_block, jnp.where(charge == 1, near_block, far_block))


def shards(wavefunction, left_env, right_env, coupling, sec_size):
    sector_width = wavefunction.shape[-1]
    pair_index = lax.axis_index("chan")
    sector = lax.axis_index("panel")
    charge = pick_entry(jnp.array(CHARGE_TABLE, jnp.int32), pair_index)
    keep_mask = block_mask(sec_size, sector, charge, sector_width)
    masked = jnp.where(keep_mask, wavefunction[0, 0], jnp.zeros((), jnp.bfloat16))
    same_coef, raise_coef = coupling_masks(coupling)
    near_right = from_behind(right_env, "panel", -1)
    far_right = from_behind(right_env, "panel", -2)
    right_here = choose_block(charge, right_env[:, 0], near_right[:, 0], far_right[:, 0])
    lower = from_behind(masked, "panel", 1)
    pair_here, pair_lower = (
        lax.all_gather(masked[None], "chan", axis=0, tiled=True),
        lax.all_gather(lower[None], "chan", axis=0, tiled=True),
    )
    plan_tables = (
        ((0, 0, 0, 0), (0, 1, 2, 3), (1, 1, 1, 1)),
        ((1, 0, 0, 0), (2, 2, 1, 3), (1, 1, 1, 0)),
        ((1, 1, 1, 1), (1, 3, 3, 3), (1, 1, 1, 1)),
    )
    summed_total = jnp.zeros((sector_width, sector_width), jnp.float32)
    for channel_table, partner_table, flag_table in plan_tables:
        channel = pick_entry(jnp.array(channel_table, jnp.int32), pair_index)
        partner = pick_entry(jnp.array(partner_table, jnp.int32), pair_index)
        active = pick_entry(jnp.array(flag_table, jnp.int32), pair_index)
        source = jnp.where(channel == 0, pair_here, pair_lower)
        coef_matrix = jnp.where(channel == 0, same_coef, raise_coef)
        panel_block = lax.dynamic_index_in_dim(source, partner, 0, keepdims=False)
        left_block = lax.dynamic_index_in_dim(left_env[:, 0], channel, 0, keepdims=False)
        right_block = lax.dynamic_index_in_dim(right_here, channel, 0, keepdims=False)
        weight = pick_entry(
            pick_column(jnp.transpose(coef_matrix), pair_index), partner
        ) * active.astype(jnp.float32)
        product = jnp.dot(left_block, panel_block, preferred_element_type=jnp.float32).astype(
            jnp.bfloat16
        )
        summed_total = summed_total + weight * outer_dot(product, right_block)
    applied = jnp.where(keep_mask, summed_total, 0.0).astype(jnp.bfloat16)
    return applied[None, None]


def solution(mesh):
    return jax.shard_map(
        shards,
        mesh=mesh,
        in_specs=(
            P("chan", "panel", None, None),
            P(None, "panel", None, None),
            P(None, "panel", None, None),
            P(),
            P(),
        ),
        out_specs=P("chan", "panel", None, None),
        check_vma=False,
    )
```

profile of v0, /device:TPU:0, one launch (start us, length us, event | category | flops | bytes accessed | tf_op | source)
XLA Modules:
  0.0 181.7 jit_solution(8142304349341767632)
XLA Ops:
  6.5 0.0 copy-start
  6.5 0.0 all-gather.4.cloned.1.call-start
  6.5 1.4 select_reduce_fusion.9
  8.6 1.4 fusion.42
  10.0 1.3 iota_compare_fusion
  11.3 2.8 %and_select_fusion = bf16[1,768,768]{2,1,0:T(8,128)(2,1)} fusion(bf16[1,1,768,768]{3,2,1,0:T(8,128)(2,1)} %param.16, pred[]{:T(512)S(6)} %lt.52, pred[768]{0:T(1024)(128)(4,1)S(1)} %get-tuple-element.14, pred[768]{0:T(1024)(128)(4,1)S(1)} %get-tuple-element.15), kind=kLoop, calls=%fused_computation.2 | loop fusion | flops 1769472 | bytes 2360833 | tf_op jit(solution)/shard_map/jit(_where)/select_n | solution.py:60
  14.1 0.0 copy-start.1
  14.1 0.0 copy-start.4
  14.1 0.0 copy-start.5
  14.1 0.0 all-gather.4.cloned.1.call-update
  14.2 0.0 all-gather.6.cloned.1.call-start
  14.2 0.0 copy-done
  14.2 0.5 fusion
  14.7 5.1 %collective-permute-start = (bf16[768,768]{1,0:T(8,128)(2,1)S(1)}, bf16[768,768]{1,0:T(8,128)(2,1)S(1)}, u32[]{:S(2)}, u32[]{:S(2)}) collective-permute-start(bf16[768,768]{1,0:T(8,128)(2,1)S(1)} %fusion), channel_id=1, source_target_pairs={{0,4},{4,8},{8,12},{12,16},{16,20},{20,24},{24,28},{1,5},{5,9},{9,... | collective-permute-start | bytes 3538952 | tf_op jit(solution)/shard_map/ppermute | solution.py:12
  19.8 25.1 %collective-permute-done = bf16[768,768]{1,0:T(8,128)(2,1)S(1)} collective-permute-done((bf16[768,768]{1,0:T(8,128)(2,1)S(1)}, bf16[768,768]{1,0:T(8,128)(2,1)S(1)}, u32[]{:S(2)}, u32[]{:S(2)}) %collective-permute-start) | collective-permute-done | bytes 1179680 | tf_op jit(solution)/shard_map/ppermute | solution.py:12
  44.9 0.0 copy-start.3
  44.9 1.0 copy-done.3
  45.9 0.0 all-gather.6.cloned.1.call-update
  46.0 0.0 copy-done.1
  46.0 1.3 collective-permute-start.1
  47.3 1.3 collective-permute-start.2
  49.2 1.4 select_reduce_fusion.3
  51.7 0.6 select_reduce_fusion.8
  55.3 1.3 select_reduce_fusion.6
  61.0 1.3 select_reduce_fusion.4
  63.0 0.0 copy-done.4
  63.0 0.0 copy-done.5
  63.0 0.8 select_reduce_fusion.1
  63.8 1.2 fusion.44
  65.6 1.2 fusion.46
  70.5 1.2 fusion.45
  72.4 28.5 %collective-permute-done.1 = bf16[2,1,768,768]{3,2,1,0:T(8,128)(2,1)} collective-permute-done((bf16[2,1,768,768]{3,2,1,0:T(8,128)(2,1)S(1)}, bf16[2,1,768,768]{3,2,1,0:T(8,128)(2,1)}, u32[]{:S(2)}, u32[]{:S(2)}) %collective-permute-start.1) | collective-permute-done | bytes 2359328 | tf_op jit(solution)/shard_map/ppermute | solution.py:12
  100.9 51.7 %collective-permute-done.2 = bf16[2,1,768,768]{3,2,1,0:T(8,128)(2,1)} collective-permute-done((bf16[2,1,768,768]{3,2,1,0:T(8,128)(2,1)S(1)}, bf16[2,1,768,768]{3,2,1,0:T(8,128)(2,1)}, u32[]{:S(2)}, u32[]{:S(2)}) %collective-permute-start.2) | collective-permute-done | bytes 2359328 | tf_op jit(solution)/shard_map/ppermute | solution.py:12
  152.7 3.7 %select_select_fusion = bf16[2,1,768,768]{3,2,1,0:T(8,128)(2,1)} fusion(bf16[2,1,768,768]{3,2,1,0:T(8,128)(2,1)S(1)} %copy-done.1, bf16[2,1,768,768]{3,2,1,0:T(8,128)(2,1)} %collective-permute-done.1, bf16[2,1,768,768]{3,2,1,0:T(8,128)(2,1)} %collective-permute-done.2, pred[]{:T(512)S(6)} %eq.122, pred[]{:T(512)S(6)} %eq.121), kind=kLoop, calls=%fused_computation.1 | loop fusion | flops 2359296 | bytes 9437186 | tf_op jit(solution)/shard_map/jit(_where)/select_n | solution.py:51
  156.3 0.0 copy-start.2
  156.3 0.0 all-gather.4.cloned.1.call-done
  156.4 6.1 %fusion.8 = f32[768,768]{1,0:T(8,128)} fusion(bf16[2,1,768,768]{3,2,1,0:T(8,128)(2,1)} %select_select_fusion, bf16[2,1,768,768]{3,2,1,0:T(8,128)(2,1)} %param.17, bf16[4,768,768]{2,1,0:T(8,128)(2,1)} %all-gather.4.cloned.1.call-done, s32[]{:T(128)S(6)} %select_n.181), kind=kOutput, calls=%fused_computation.16 | convolution fusion | flops 1812529152 | bytes 5898244 | tf_op jit(solution)/shard_map/dot_general | solution.py:26
  162.5 0.0 all-gather.6.cloned.1.call-done
  162.5 0.0 copy-done.2
  162.5 5.6 %fusion.11 = f32[768,768]{1,0:T(8,128)} fusion(bf16[2,1,768,768]{3,2,1,0:T(8,128)(2,1)S(1)} %copy-done.2, s32[]{:T(128)S(6)} %select_n.193, bf16[4,768,768]{2,1,0:T(8,128)(2,1)} %bitcast.60, s32[]{:T(128)S(6)} %select_n.196, bf16[4,768,768]{2,1,0:T(8,128)(2,1)} %all-gather.4.cloned.1.call-done, bf16[2,1,768,768]{3,2,1,0:T(8,128)(2,1)} %param.17, pred[]{:T(512)S(6)} %eq.125), kind=kOutput, calls=%fused_computation.19 | convolution fusion | flops 1813118976 | bytes 7079936 | tf_op jit(solution)/shard_map/dot_general | solution.py:26
  168.1 6.8 %fusion.1 = bf16[1,1,768,768]{3,2,1,0:T(8,128)(2,1)} fusion(f32[768,768]{1,0:T(8,128)} %fusion.11, f32[768,768]{1,0:T(8,128)} %fusion.8, bf16[2,1,768,768]{3,2,1,0:T(8,128)(2,1)S(1)} %copy-done.2, s32[]{:T(128)S(6)} %select_n.204, f32[]{:T(128)S(6)} %mul.33, f32[]{:T(128)S(6)} %mul.30, f32[]{:T(128)S(6)} %mul.27, pred[]{:T(512)S(6)} %lt.52, ...), kind=kOutput, calls=%fused_computation.8 | convolution fusion | flops 1818427392 | bytes 10622976 | tf_op jit(solution)/shard_map/dot_general | solution.py:26
  (1 shorter events, 0.0 us)
Async XLA Ops:
  6.5 7.7 %copy-start = (bf16[1,1,768,768]{3,2,1,0:T(8,128)(2,1)S(1)}, bf16[1,1,768,768]{3,2,1,0:T(8,128)(2,1)}, u32[]{:S(2)}) copy-start(bf16[1,1,768,768]{3,2,1,0:T(8,128)(2,1)} %param.16) | copy-start | bytes 3538948
  6.5 149.8 %all-gather.4.cloned.1.call-start = ((), (), s32[]{:S(2)}) async-start(), calls=%async_computation | async-start | bytes 5898240 | tf_op jit(solution)/shard_map/all_gather | solution.py:67
  14.1 31.8 %copy-start.1 = (bf16[2,1,768,768]{3,2,1,0:T(8,128)(2,1)S(1)}, bf16[2,1,768,768]{3,2,1,0:T(8,128)(2,1)}, u32[]{:S(2)}) copy-start(bf16[2,1,768,768]{3,2,1,0:T(8,128)(2,1)} %param.18) | copy-start | bytes 7077892
  14.1 48.9 %copy-start.4 = (f32[2,4,4]{2,1,0:T(4,128)S(1)}, f32[2,4,4]{2,1,0:T(4,128)}, u32[]{:S(2)}) copy-start(f32[2,4,4]{2,1,0:T(4,128)} %param.19) | copy-start | bytes 388
  14.1 48.9 %copy-start.5 = (s32[4]{0:T(128)S(1)}, s32[4]{0:T(128)}, u32[]{:S(2)}) copy-start(s32[4]{0:T(128)} %constant.69.clone) | copy-start | bytes 52
  14.2 148.3 %all-gather.6.cloned.1.call-start = ((), (), s32[]{:S(2)}) async-start(), calls=%async_computation.1 | async-start | bytes 5898240 | tf_op jit(solution)/shard_map/all_gather | solution.py:68
  14.7 30.2 %collective-permute-start = (bf16[768,768]{1,0:T(8,128)(2,1)S(1)}, bf16[768,768]{1,0:T(8,128)(2,1)S(1)}, u32[]{:S(2)}, u32[]{:S(2)}) collective-permute-start(bf16[768,768]{1,0:T(8,128)(2,1)S(1)} %fusion), channel_id=1, source_target_pairs={{0,4},{4,8},{8,12},{12,16},{16,20},{20,24},{24,28},{1,5},{5,9},{9,... | collective-permute-start | bytes 3538952 | tf_op jit(solution)/shard_map/ppermute | solution.py:12
  44.9 1.0 copy-start.3
  46.0 55.0 %collective-permute-start.1 = (bf16[2,1,768,768]{3,2,1,0:T(8,128)(2,1)S(1)}, bf16[2,1,768,768]{3,2,1,0:T(8,128)(2,1)}, u32[]{:S(2)}, u32[]{:S(2)}) collective-permute-start(bf16[2,1,768,768]{3,2,1,0:T(8,128)(2,1)S(1)} %copy-done.1), channel_id=1, source_target_pairs={{4,0},{8,4},{12,8},{16,12},{20,16},{24,20},{28,24},{5,1},{9,5},{13... | collective-permute-start | bytes 7077896 | tf_op jit(solution)/shard_map/ppermute | solution.py:12
  47.3 105.4 %collective-permute-start.2 = (bf16[2,1,768,768]{3,2,1,0:T(8,128)(2,1)S(1)}, bf16[2,1,768,768]{3,2,1,0:T(8,128)(2,1)}, u32[]{:S(2)}, u32[]{:S(2)}) collective-permute-start(bf16[2,1,768,768]{3,2,1,0:T(8,128)(2,1)S(1)} %copy-done.1), channel_id=1, source_target_pairs={{8,0},{12,4},{16,8},{20,12},{24,16},{28,20},{9,1},{13,5},{17,9},{2... | collective-permute-start | bytes 7077896 | tf_op jit(solution)/shard_map/ppermute | solution.py:12
  156.3 6.2 %copy-start.2 = (bf16[2,1,768,768]{3,2,1,0:T(8,128)(2,1)S(1)}, bf16[2,1,768,768]{3,2,1,0:T(8,128)(2,1)}, u32[]{:S(2)}) copy-start(bf16[2,1,768,768]{3,2,1,0:T(8,128)(2,1)} %select_select_fusion) | copy-start | bytes 7077892
Sparse Core Ops, SparseCore 0:
  14.3 40.1 all-gather.3
  56.0 37.4 all-gather.5
where the time goes:
time: 182 us
  waiting for transfers between devices  105 us (58%)
  between operations  28.8 us (16%)
  other arithmetic  20.2 us (11%)
  matrix products  18.5 us (10%)
  starting transfers between devices  7.7 us (4%)
    ppermute x3, waiting for transfers between devices, from_behind(): return lax.ppermute(block, axis, route)  105 us
    dot_general x3, matrix products, outer_dot(): lax.dot_general(left_matrix, right_matrix, (((1,), (1,)), ((), ())), pref...  18.5 us
    reduce_sum x9, other arithmetic, pick_entry(): jnp.sum(jnp.where(slot_ids == position, lookup_table, jnp.zeros_like(look...  11.2 us
    ppermute x3, starting transfers between devices, from_behind(): return lax.ppermute(block, axis, route)  7.66 us
    select_n x1, other arithmetic, choose_block(): jnp.where(charge == 0, own_block, jnp.where(charge == 1, near_block, far_...  3.67 us
  transfers between devices with their start and end apart: 5, of which 3 were waited for; matrix products, arithmetic and copies ran while one was open for 11% of the time, Pallas kernels for 0%

commit v1 on v0

v1 whole, which is shorter than its diff:
```python
import functools

import jax
import jax.numpy as jnp
from jax import lax
from jax.experimental import pallas as pl
from jax.experimental.pallas import tpu as pltpu
from jax.sharding import PartitionSpec as P

MESH = pl.DeviceIdType.MESH
STEP = 128
ROWS = 256
BF16 = jnp.bfloat16


def dot(a, b):
    return jnp.dot(a, b, preferred_element_type=jnp.float32)


def outer_dot(a, b):
    return lax.dot_general(a, b, (((1,), (1,)), ((), ())), preferred_element_type=jnp.float32)


def inside(shape, row0, col0, rows_live, cols_live):
    row = lax.broadcasted_iota(jnp.int32, shape, 0) + row0
    col = lax.broadcasted_iota(jnp.int32, shape, 1) + col0
    return jnp.logical_and(row < rows_live, col < cols_live)


def kernel(
    sectors,
    coupling,
    sec_size,
    psi_hbm,
    left_hbm,
    right_hbm,
    out,
    left,
    right,
    own,
    in_psi,
    in_right,
    in_part,
    out_part,
    mix_a,
    mix_b,
    mix_c,
    half_a,
    half_b,
    acc,
    local_sem,
    psi_send,
    psi_recv,
    right_send,
    right_recv,
    part_send,
    part_recv,
):
    width = own.shape[0]
    steps = width // STEP
    p = lax.axis_index("panel")
    pair = lax.axis_index("chan")
    last = sectors - 1

    psi_src = psi_hbm.at[0, 0]
    left_copies = [
        pltpu.make_async_copy(left_hbm.at[k, 0], left.at[k], local_sem.at[k]) for k in range(2)
    ]
    right_copies = [
        pltpu.make_async_copy(right_hbm.at[k, 0], right.at[k], local_sem.at[2 + k])
        for k in range(2)
    ]
    own_copy = pltpu.make_async_copy(psi_src, own, local_sem.at[4])

    def live(sector):
        exists = jnp.logical_and(sector >= 0, sector < sectors)
        return jnp.where(exists, sec_size[jnp.clip(sector, 0, last)], 0)

    def rows_at(ref, c, n=STEP):
        return ref.at[pl.ds(pl.multiple_of(c * n, n), n), :]

    def remote(src, dst, send, recv, panel, chan):
        return pltpu.make_async_remote_copy(
            src_ref=src,
            dst_ref=dst,
            send_sem=send,
            recv_sem=recv,
            device_id={"panel": panel, "chan": chan},
            device_id_type=MESH,
        )

    def psi_copy(src, c, panel, chan):
        return remote(rows_at(src, c), rows_at(in_psi, c), psi_send.at[c], psi_recv.at[c], panel, chan)

    def right_copy(k, c, panel, chan):
        src = rows_at(right_hbm.at[k, 0], c)
        return remote(src, rows_at(in_right, c), right_send.at[c], right_recv.at[c], panel, chan)

    def part_copy(c, panel, chan):
        return remote(
            out_part.at[c], in_part.at[c], part_send.at[c], part_recv.at[c], panel, chan
        )

    def each(body, n=None):
        def step(c, carry):
            body(c)
            return carry

        lax.fori_loop(0, steps if n is None else n, step, 0)

    def multiply(dst, a, b):
        def body(r):
            at = pl.ds(pl.multiple_of(r * ROWS, ROWS), ROWS)
            dst[at, :] = dot(a[at, :], b[...]).astype(BF16)

        each(body, width // ROWS)

    def mask_block(dst, src, rows_live, cols_live):
        def body(c):
            at = pl.ds(pl.multiple_of(c * STEP, STEP), STEP)
            block = src[at, :]
            keep = inside(block.shape, c * STEP, 0, rows_live, cols_live)
            dst[at, :] = jnp.where(keep, block.astype(jnp.float32), 0.0).astype(BF16)

        each(body)

    def write_out(c, value, rows_live, cols_live):
        at = pl.ds(pl.multiple_of(c * STEP, STEP), STEP)
        keep = inside(value.shape, 0, c * STEP, rows_live, cols_live)
        out[0, 0, :, at] = jnp.where(keep, value, 0.0).astype(BF16)

    def write_zeros():
        out[...] = jnp.zeros_like(out)

    @pl.when(pair != 2)
    def _():
        left_copies[0].start()
        own_copy.start()

    @pl.when(jnp.logical_or(pair == 0, pair == 2))
    def _():
        left_copies[1].start()

    @pl.when(pair == 0)
    def _():
        right_copies[0].start()
        right_copies[1].start()

    barrier = pltpu.get_barrier_semaphore()
    partners = (
        (0, p >= 1, -1, 1),
        (1, p < last, 1, 0),
        (1, p < last, 0, 2),
        (2, p < last, 0, 1),
        (2, jnp.logical_and(p >= 1, p < last), -1, 3),
        (2, p >= 1, -1, 2),
        (2, p < last, 1, 2),
        (3, p < last - 1, 1, 2),
        (3, p < last - 1, 2, 3),
        (3, p >= 2, -2, 3),
    )
    for role, meets, shift, chan in partners:

        @pl.when(jnp.logical_and(pair == role, meets))
        def _(shift=shift, chan=chan):
            pl.semaphore_signal(
                barrier, inc=1, device_id={"panel": p + shift, "chan": chan}, device_id_type=MESH
            )

    met = sum(
        jnp.where(jnp.logical_and(pair == role, meets), 1, 0) for role, meets, _, _ in partners
    )

    @pl.when(met > 0)
    def _():
        pl.semaphore_wait(barrier, met)

    @pl.when(pair == 0)
    def _pair0():
        @pl.when(p >= 1)
        def _():
            each(lambda c: right_copy(0, c, p - 1, 1).start())

        left_copies[0].wait()
        own_copy.wait()
        rows_live, cols_live = live(p), live(p)
        mask_block(own, own, rows_live, cols_live)
        multiply(half_a, left.at[0], own)
        right_copies[0].wait()
        weight = coupling[0, 0, 0]

        def kept(c):
            acc[c] = weight * outer_dot(half_a[...], right[0, pl.ds(pl.multiple_of(c * STEP, STEP), STEP), :])

        each(kept)
        right_copies[1].wait()
        left_copies[1].wait()

        @pl.when(p >= 1)
        def _():
            def fold(c):
                psi_copy(in_psi, c, p - 1, 1).wait_recv()
                at = pl.ds(pl.multiple_of(c * STEP, STEP), STEP)
                half_b[at, :] = outer_dot(in_psi[at, :], right[1]).astype(BF16)

            each(fold)

            def finish(c):
                at = pl.ds(pl.multiple_of(c * STEP, STEP), STEP)
                write_out(c, acc[c] + dot(left[1], half_b[:, at]), rows_live, cols_live)

            each(finish)
            each(lambda c: right_copy(0, c, p - 1, 1).wait_send())

        @pl.when(p == 0)
        def _():
            each(lambda c: write_out(c, acc[c], rows_live, cols_live))

    @pl.when(pair == 1)
    def _pair1():
        left_copies[0].wait()
        own_copy.wait()

        @pl.when(p == last)
        def _():
            write_zeros()

        @pl.when(p < last)
        def _():
            rows_live, cols_live = live(p), live(p + 1)

            def mix(c):
                psi_copy(in_psi, c, p, 2).wait_recv()
                at = pl.ds(pl.multiple_of(c * STEP, STEP), STEP)
                mine = own[at, :].astype(jnp.float32)
                theirs = in_psi[at, :].astype(jnp.float32)
                keep = inside(mine.shape, c * STEP, 0, rows_live, cols_live)

                def blend(x, y):
                    return jnp.where(keep, x * mine + y * theirs, 0.0).astype(BF16)

                mix_a[at, :] = blend(coupling[1, 0, 1], coupling[1, 0, 2])
                psi_copy(mix_a, c, p + 1, 0).start()
                mix_b[at, :] = blend(coupling[0, 1, 1], coupling[0, 1, 2])
                mix_c[at, :] = blend(coupling[0, 2, 1], coupling[0, 2, 2])

            each(mix)
            multiply(half_b, left.at[0], mix_c)
            multiply(half_a, left.at[0], mix_b)

            def kept(c):
                right_copy(0, c, p + 1, 0).wait_recv()
                block = in_right[pl.ds(pl.multiple_of(c * STEP, STEP), STEP), :]
                out_part[c] = outer_dot(half_b[...], block).astype(BF16)
                part_copy(c, p, 2).start()
                acc[c] = outer_dot(half_a[...], block)

            each(kept)

            def finish(c):
                part_copy(c, p, 2).wait_recv()
                moved = coupling[1, 1, 3] * in_part[c].astype(jnp.float32)
                write_out(c, acc[c] + moved, rows_live, cols_live)

            each(finish)
            each(lambda c: psi_copy(mix_a, c, p + 1, 0).wait_send())
            each(lambda c: part_copy(c, p, 2).wait_send())

    @pl.when(pair == 2)
    def _pair2():
        @pl.when(p < last)
        def _():
            each(lambda c: psi_copy(psi_src, c, p, 1).start())

        left_copies[1].wait()

        @pl.when(jnp.logical_and(p >= 1, p < last))
        def _():
            each(lambda c: psi_copy(in_psi, c, p - 1, 3).wait_recv())

        @pl.when(p >= 1)
        def _():
            each(lambda c: right_copy(1, c, p - 1, 2).start())

        @pl.when(p == last)
        def _():
            write_zeros()

        @pl.when(p < last)
        def _():
            rows_live, cols_live = live(p), live(p + 1)

            @pl.when(p >= 1)
            def _():
                mask_block(mix_a, in_psi, live(p - 1), live(p + 1))

            @pl.when(p == 0)
            def _():
                mix_a[...] = jnp.zeros_like(mix_a)

            multiply(half_a, left.at[1], mix_a)

            def moved(c):
                right_copy(1, c, p + 1, 2).wait_recv()
                block = in_right[pl.ds(pl.multiple_of(c * STEP, STEP), STEP), :]
                value = outer_dot(half_a[...], block)
                out_part[c] = value.astype(BF16)
                part_copy(c, p, 1).start()
                acc[c] = coupling[1, 2, 3] * value

            each(moved)

            def finish(c):
                part_copy(c, p, 1).wait_recv()
                write_out(c, acc[c] + in_part[c].astype(jnp.float32), rows_live, cols_live)

            each(finish)
            each(lambda c: psi_copy(psi_src, c, p, 1).wait_send())
            each(lambda c: part_copy(c, p, 1).wait_send())

        @pl.when(p >= 1)
        def _():
            each(lambda c: right_copy(1, c, p - 1, 2).wait_send())

    @pl.when(pair == 3)
    def _pair3():
        @pl.when(p < last - 1)
        def _():
            each(lambda c: psi_copy(psi_src, c, p + 1, 2).start())

        @pl.when(p >= 2)
        def _():
            each(lambda c: right_copy(0, c, p - 2, 3).start())

        left_copies[0].wait()
        own_copy.wait()

        @pl.when(p >= last - 1)
        def _():
            write_zeros()

        @pl.when(p < last - 1)
        def _():
            rows_live, cols_live = live(p), live(p + 2)
            mask_block(own, own, rows_live, cols_live)
            multiply(half_a, left.at[0], own)

            def kept(c):
                right_copy(0, c, p + 2, 3).wait_recv()
                block = in_right[pl.ds(pl.multiple_of(c * STEP, STEP), STEP), :]
                value = coupling[0, 3, 3] * outer_dot(half_a[...], block)
                write_out(c, value, rows_live, cols_live)

            each(kept)
            each(lambda c: psi_copy(psi_src, c, p + 1, 2).wait_send())

        @pl.when(p >= 2)
        def _():
            each(lambda c: right_copy(0, c, p - 2, 3).wait_send())


def shards(sectors, wavefunction, left_env, right_env, coupling, sec_size):
    width = wavefunction.shape[-1]
    steps = width // STEP
    square = pltpu.VMEM((width, width), BF16)
    strips = (steps, width, STEP)
    return pl.pallas_call(
        functools.partial(kernel, sectors),
        out_shape=jax.ShapeDtypeStruct(wavefunction.shape, BF16),
        in_specs=[pl.BlockSpec(memory_space=pltpu.SMEM)] * 2
        + [pl.BlockSpec(memory_space=pl.ANY)] * 3,
        out_specs=pl.BlockSpec(memory_space=pltpu.VMEM),
        scratch_shapes=[
            pltpu.VMEM((2, width, width), BF16),
            pltpu.VMEM((2, width, width), BF16),
            square,
            square,
            square,
            pltpu.VMEM(strips, BF16),
            pltpu.VMEM(strips, BF16),
            square,
            square,
            square,
            square,
            square,
            pltpu.VMEM(strips, jnp.float32),
            pltpu.SemaphoreType.DMA((5,)),
        ]
        + [pltpu.SemaphoreType.DMA((steps,))] * 6,
        compiler_params=pltpu.CompilerParams(
            collective_id=0, has_side_effects=True, vmem_limit_bytes=48 * 1024 * 1024
        ),
    )(coupling, sec_size, wavefunction, left_env, right_env)


def solution(mesh):
    sectors = mesh.shape["panel"]
    return jax.shard_map(
        functools.partial(shards, sectors),
        mesh=mesh,
        in_specs=(
            P("chan", "panel", None, None),
            P(None, "panel", None, None),
            P(None, "panel", None, None),
            P(),
            P(),
        ),
        out_specs=P("chan", "panel", None, None),
        check_vma=False,
    )
```

time: 182 us -> 45.1 us (0.25)
  the two profiles are of different devices: /device:TPU:0 before, /device:TPU:13 now
where the time goes in v1:
time: 45.1 us; the launch traced here: 44.8 us
  Pallas kernels  39.5 us (88%)
  local copies, waits for them, and re-layouts  5.29 us (12%)
    pallas_call x1, Pallas kernels, shards(): pl.pallas_call(functools.partial(kernel, sectors), out_shape=jax.ShapeDty...  39.5 us
    unnamed x9, local copies, waits for them, and re-layouts  5.29 us

profile of v1, /device:TPU:13, one launch (start us, length us, event | category | flops | bytes accessed | tf_op | source)
XLA Modules:
  0.0 44.8 jit_solution(12516457014920846641)
XLA Ops:
  0.0 0.0 copy-start
  0.0 1.7 %copy-done = bf16[2,1,768,768]{3,2,1,0:T(8,128)(2,1)S(1)} copy-done((bf16[2,1,768,768]{3,2,1,0:T(8,128)(2,1)S(1)}, bf16[2,1,768,768]{3,2,1,0:T(8,128)(2,1)}, u32[]{:S(2)}) %copy-start) | copy-done | bytes 2359320
  1.7 0.0 copy-start.1
  1.7 1.3 %copy-done.1 = bf16[1,1,768,768]{3,2,1,0:T(8,128)(2,1)S(1)} copy-done((bf16[1,1,768,768]{3,2,1,0:T(8,128)(2,1)S(1)}, bf16[1,1,768,768]{3,2,1,0:T(8,128)(2,1)}, u32[]{:S(2)}) %copy-start.1) | copy-done | bytes 1179672
  2.9 0.0 copy-start.2
  2.9 0.7 %copy-done.2 = f32[2,4,4]{2,1,0:T(4,128)S(1)} copy-done((f32[2,4,4]{2,1,0:T(4,128)S(1)}, f32[2,4,4]{2,1,0:T(4,128)}, u32[]{:S(2)}) %copy-start.2) | copy-done | bytes 152
  3.6 0.0 copy-start.3
  3.6 0.7 %copy-done.3 = s32[8]{0:T(128)S(1)} copy-done((s32[8]{0:T(128)S(1)}, s32[8]{0:T(128)}, u32[]{:S(2)}) %copy-start.3) | copy-done | bytes 56
  4.3 39.5 %shard_map.55 = bf16[1,1,768,768]{3,2,1,0:T(8,128)(2,1)S(1)} custom-call(f32[2,4,4]{2,1,0:T(4,128)S(1)} %copy-done.2, s32[8]{0:T(128)S(1)} %copy-done.3, bf16[1,1,768,768]{3,2,1,0:T(8,128)(2,1)S(1)} %copy-done.1, bf16[2,1,768,768]{3,2,1,0:T(8,128)(2,1)S(1)} %copy-done, bf16[2,1,768,768]{3,2,1,0:T(8,128)(2,1)} %right_hbm.1), custom_call_target="tpu_custom_call" | custom-call | tf_op jit(solution)/shard_map/pallas_call | solution.py:367
  43.7 1.0 %copy.7 = bf16[1,1,768,768]{3,2,1,0:T(8,128)(2,1)} copy(bf16[1,1,768,768]{3,2,1,0:T(8,128)(2,1)S(1)} %shard_map.55) | data formatting | bytes 2359296
Async XLA Ops:
  0.0 1.7 %copy-start = (bf16[2,1,768,768]{3,2,1,0:T(8,128)(2,1)S(1)}, bf16[2,1,768,768]{3,2,1,0:T(8,128)(2,1)}, u32[]{:S(2)}) copy-start(bf16[2,1,768,768]{3,2,1,0:T(8,128)(2,1)} %left_hbm.1) | copy-start | bytes 7077892
  1.7 1.3 %copy-start.1 = (bf16[1,1,768,768]{3,2,1,0:T(8,128)(2,1)S(1)}, bf16[1,1,768,768]{3,2,1,0:T(8,128)(2,1)}, u32[]{:S(2)}) copy-start(bf16[1,1,768,768]{3,2,1,0:T(8,128)(2,1)} %psi_hbm.1) | copy-start | bytes 3538948
  2.9 0.7 %copy-start.2 = (f32[2,4,4]{2,1,0:T(4,128)S(1)}, f32[2,4,4]{2,1,0:T(4,128)}, u32[]{:S(2)}) copy-start(f32[2,4,4]{2,1,0:T(4,128)} %coupling.1) | copy-start | bytes 388
  3.6 0.7 %copy-start.3 = (s32[8]{0:T(128)S(1)}, s32[8]{0:T(128)}, u32[]{:S(2)}) copy-start(s32[8]{0:T(128)} %sec_size.1) | copy-start | bytes 100

commit v2 on v1

--- a/solution.py
+++ b/solution.py
@@ -29,8 +29,8 @@
 
 def kernel(
     sectors,
-    coupling,
-    sec_size,
+    coupling_hbm,
+    sec_size_hbm,
     psi_hbm,
     left_hbm,
     right_hbm,
@@ -48,6 +48,8 @@
     half_a,
     half_b,
     acc,
+    coupling,
+    sec_size,
     local_sem,
     psi_send,
     psi_recv,
@@ -58,6 +60,7 @@
 ):
     width = own.shape[0]
     steps = width // STEP
+    early = steps // 2
     p = lax.axis_index("panel")
     pair = lax.axis_index("chan")
     last = sectors - 1
@@ -71,6 +74,10 @@
         for k in range(2)
     ]
     own_copy = pltpu.make_async_copy(psi_src, own, local_sem.at[4])
+    coupling_copy = pltpu.make_async_copy(coupling_hbm, coupling, local_sem.at[5])
+    size_copy = pltpu.make_async_copy(sec_size_hbm, sec_size, local_sem.at[6])
+    coupling_copy.start()
+    size_copy.start()
 
     def live(sector):
         exists = jnp.logical_and(sector >= 0, sector < sectors)
@@ -175,6 +182,9 @@
     def _():
         pl.semaphore_wait(barrier, met)
 
+    coupling_copy.wait()
+    size_copy.wait()
+
     @pl.when(pair == 0)
     def _pair0():
         @pl.when(p >= 1)
@@ -276,11 +286,15 @@
 
         @pl.when(jnp.logical_and(p >= 1, p < last))
         def _():
-            each(lambda c: psi_copy(in_psi, c, p - 1, 3).wait_recv())
+            each(lambda c: psi_copy(in_psi, c, p - 1, 3).wait_recv(), early)
 
         @pl.when(p >= 1)
         def _():
             each(lambda c: right_copy(1, c, p - 1, 2).start())
+
+        @pl.when(jnp.logical_and(p >= 1, p < last))
+        def _():
+            each(lambda c: psi_copy(in_psi, c + early, p - 1, 3).wait_recv(), steps - early)
 
         @pl.when(p == last)
         def _():
@@ -367,8 +381,7 @@
     return pl.pallas_call(
         functools.partial(kernel, sectors),
         out_shape=jax.ShapeDtypeStruct(wavefunction.shape, BF16),
-        in_specs=[pl.BlockSpec(memory_space=pltpu.SMEM)] * 2
-        + [pl.BlockSpec(memory_space=pl.ANY)] * 3,
+        in_specs=[pl.BlockSpec(memory_space=pl.ANY)] * 5,
         out_specs=pl.BlockSpec(memory_space=pltpu.VMEM),
         scratch_shapes=[
             pltpu.VMEM((2, width, width), BF16),
@@ -384,11 +397,13 @@
             square,
             square,
             pltpu.VMEM(strips, jnp.float32),
-            pltpu.SemaphoreType.DMA((5,)),
+            pltpu.SMEM(coupling.shape, coupling.dtype),
+            pltpu.SMEM(sec_size.shape, sec_size.dtype),
+            pltpu.SemaphoreType.DMA((7,)),
         ]
         + [pltpu.SemaphoreType.DMA((steps,))] * 6,
         compiler_params=pltpu.CompilerParams(
-            collective_id=0, has_side_effects=True, vmem_limit_bytes=48 * 1024 * 1024
+            collective_id=0, has_side_effects=True, vmem_limit_bytes=56 * 1024 * 1024
         ),
     )(coupling, sec_size, wavefunction, left_env, right_env)
 

time: 45.1 us -> 40 us (0.89)
  local copies, waits for them, and re-layouts: 5.29 us -> 2.36 us
  Pallas kernels: 39.5 us -> 37.4 us
    unnamed x9 -> x1, local copies, waits for them, and re-layouts: 5.29 us -> 2.36 us
    pallas_call x1, Pallas kernels: 39.5 us -> 37.4 us  [shards(): pl.pallas_call(functools.partial(kernel, sectors), out_shape=jax.ShapeDty...]
where the time goes in v2:
time: 40 us; the launch traced here: 39.8 us
  Pallas kernels  37.4 us (94%)
  local copies, waits for them, and re-layouts  2.36 us (6%)
    pallas_call x1, Pallas kernels, shards(): pl.pallas_call(functools.partial(kernel, sectors), out_shape=jax.ShapeDty...  37.4 us
    unnamed x1, local copies, waits for them, and re-layouts  2.36 us

profile of v2, /device:TPU:13, one launch (start us, length us, event | category | flops | bytes accessed | tf_op | source)
XLA Modules:
  0.0 39.8 jit_solution(1699942932591771818)
XLA Ops:
  0.0 37.4 %shard_map.55 = bf16[1,1,768,768]{3,2,1,0:T(8,128)(2,1)} custom-call(f32[2,4,4]{2,1,0:T(4,128)} %coupling_hbm.1, s32[8]{0:T(128)} %sec_size_hbm.1, bf16[1,1,768,768]{3,2,1,0:T(8,128)(2,1)} %psi_hbm.1, bf16[2,1,768,768]{3,2,1,0:T(8,128)(2,1)} %left_hbm.1, bf16[2,1,768,768]{3,2,1,0:T(8,128)(2,1)} %right_hbm.1), custom_call_target="tpu_custom_call" | custom-call | tf_op jit(solution)/shard_map/pallas_call | solution.py:381
  37.4 2.4 %copy.7 = bf16[1,1,768,768]{3,2,1,0:T(8,128)(2,1)} copy(bf16[1,1,768,768]{3,2,1,0:T(8,128)(2,1)} %shard_map.55) | data formatting | bytes 2359296

commit v3 on v2

--- a/solution.py
+++ b/solution.py
@@ -42,9 +42,8 @@
     in_right,
     in_part,
     out_part,
-    mix_a,
-    mix_b,
-    mix_c,
+    mixed,
+    both,
     half_a,
     half_b,
     acc,
@@ -96,8 +95,17 @@
             device_id_type=MESH,
         )
 
-    def psi_copy(src, c, panel, chan):
-        return remote(rows_at(src, c), rows_at(in_psi, c), psi_send.at[c], psi_recv.at[c], panel, chan)
+    def strip(c):
+        return pl.ds(pl.multiple_of(c * STEP, STEP), STEP)
+
+    def strip_copy(src, c, panel, chan):
+        return remote(src, in_psi.at[c], psi_send.at[c], psi_recv.at[c], panel, chan)
+
+    def psi_copy(c, panel, chan):
+        return strip_copy(psi_src.at[:, strip(c)], c, panel, chan)
+
+    def mix_copy(c, panel, chan):
+        return strip_copy(mixed.at[c], c, panel, chan)
 
     def right_copy(k, c, panel, chan):
         src = rows_at(right_hbm.at[k, 0], c)
@@ -209,15 +217,14 @@
         @pl.when(p >= 1)
         def _():
             def fold(c):
-                psi_copy(in_psi, c, p - 1, 1).wait_recv()
-                at = pl.ds(pl.multiple_of(c * STEP, STEP), STEP)
-                half_b[at, :] = outer_dot(in_psi[at, :], right[1]).astype(BF16)
+                mix_copy(c, p - 1, 1).wait_recv()
+                half_b[:, strip(c)] = dot(left[1], in_psi[c]).astype(BF16)
 
             each(fold)
 
             def finish(c):
-                at = pl.ds(pl.multiple_of(c * STEP, STEP), STEP)
-                write_out(c, acc[c] + dot(left[1], half_b[:, at]), rows_live, cols_live)
+                moved = outer_dot(half_b[...], right[1, strip(c), :])
+                write_out(c, acc[c] + moved, rows_live, cols_live)
 
             each(finish)
             each(lambda c: right_copy(0, c, p - 1, 1).wait_send())
@@ -240,23 +247,23 @@
             rows_live, cols_live = live(p), live(p + 1)
 
             def mix(c):
-                psi_copy(in_psi, c, p, 2).wait_recv()
-                at = pl.ds(pl.multiple_of(c * STEP, STEP), STEP)
-                mine = own[at, :].astype(jnp.float32)
-                theirs = in_psi[at, :].astype(jnp.float32)
-                keep = inside(mine.shape, c * STEP, 0, rows_live, cols_live)
+                psi_copy(c, p, 2).wait_recv()
+                mine = own[:, strip(c)].astype(jnp.float32)
+                theirs = in_psi[c].astype(jnp.float32)
+                keep = inside(mine.shape, 0, c * STEP, rows_live, cols_live)
 
                 def blend(x, y):
                     return jnp.where(keep, x * mine + y * theirs, 0.0).astype(BF16)
 
-                mix_a[at, :] = blend(coupling[1, 0, 1], coupling[1, 0, 2])
-                psi_copy(mix_a, c, p + 1, 0).start()
-                mix_b[at, :] = blend(coupling[0, 1, 1], coupling[0, 1, 2])
-                mix_c[at, :] = blend(coupling[0, 2, 1], coupling[0, 2, 2])
+                mixed[c] = blend(coupling[1, 0, 1], coupling[1, 0, 2])
+                mix_copy(c, p + 1, 0).start()
+                both[:, :STEP] = blend(coupling[0, 2, 1], coupling[0, 2, 2])
+                both[:, STEP:] = blend(coupling[0, 1, 1], coupling[0, 1, 2])
+                product = dot(left[0], both[...]).astype(BF16)
+                half_b[:, strip(c)] = product[:, :STEP]
+                half_a[:, strip(c)] = product[:, STEP:]
 
             each(mix)
-            multiply(half_b, left.at[0], mix_c)
-            multiply(half_a, left.at[0], mix_b)
 
             def kept(c):
                 right_copy(0, c, p + 1, 0).wait_recv()
@@ -273,28 +280,24 @@
                 write_out(c, acc[c] + moved, rows_live, cols_live)
 
             each(finish)
-            each(lambda c: psi_copy(mix_a, c, p + 1, 0).wait_send())
+            each(lambda c: mix_copy(c, p + 1, 0).wait_send())
             each(lambda c: part_copy(c, p, 2).wait_send())
 
     @pl.when(pair == 2)
     def _pair2():
         @pl.when(p < last)
         def _():
-            each(lambda c: psi_copy(psi_src, c, p, 1).start())
+            each(lambda c: psi_copy(c, p, 1).start())
 
         left_copies[1].wait()
 
         @pl.when(jnp.logical_and(p >= 1, p < last))
         def _():
-            each(lambda c: psi_copy(in_psi, c, p - 1, 3).wait_recv(), early)
+            each(lambda c: psi_copy(c, p - 1, 3).wait_recv(), early)
 
         @pl.when(p >= 1)
         def _():
             each(lambda c: right_copy(1, c, p - 1, 2).start())
-
-        @pl.when(jnp.logical_and(p >= 1, p < last))
-        def _():
-            each(lambda c: psi_copy(in_psi, c + early, p - 1, 3).wait_recv(), steps - early)
 
         @pl.when(p == last)
         def _():
@@ -306,13 +309,21 @@
 
             @pl.when(p >= 1)
             def _():
-                mask_block(mix_a, in_psi, live(p - 1), live(p + 1))
+                def raise_strip(c):
+                    @pl.when(c >= early)
+                    def _():
+                        psi_copy(c, p - 1, 3).wait_recv()
+
+                    block = in_psi[c]
+                    keep = inside(block.shape, 0, c * STEP, live(p - 1), live(p + 1))
+                    block = jnp.where(keep, block.astype(jnp.float32), 0.0).astype(BF16)
+                    half_a[:, strip(c)] = dot(left[1], block).astype(BF16)
+
+                each(raise_strip)
 
             @pl.when(p == 0)
             def _():
-                mix_a[...] = jnp.zeros_like(mix_a)
-
-            multiply(half_a, left.at[1], mix_a)
+                half_a[...] = jnp.zeros_like(half_a)
 
             def moved(c):
                 right_copy(1, c, p + 1, 2).wait_recv()
@@ -329,7 +340,7 @@
                 write_out(c, acc[c] + in_part[c].astype(jnp.float32), rows_live, cols_live)
 
             each(finish)
-            each(lambda c: psi_copy(psi_src, c, p, 1).wait_send())
+            each(lambda c: psi_copy(c, p, 1).wait_send())
             each(lambda c: part_copy(c, p, 1).wait_send())
 
         @pl.when(p >= 1)
@@ -340,7 +351,7 @@
     def _pair3():
         @pl.when(p < last - 1)
         def _():
-            each(lambda c: psi_copy(psi_src, c, p + 1, 2).start())
+            each(lambda c: psi_copy(c, p + 1, 2).start())
 
         @pl.when(p >= 2)
         def _():
@@ -366,7 +377,7 @@
                 write_out(c, value, rows_live, cols_live)
 
             each(kept)
-            each(lambda c: psi_copy(psi_src, c, p + 1, 2).wait_send())
+            each(lambda c: psi_copy(c, p + 1, 2).wait_send())
 
         @pl.when(p >= 2)
         def _():
@@ -387,13 +398,12 @@
             pltpu.VMEM((2, width, width), BF16),
             pltpu.VMEM((2, width, width), BF16),
             square,
-            square,
+            pltpu.VMEM(strips, BF16),
             square,
             pltpu.VMEM(strips, BF16),
             pltpu.VMEM(strips, BF16),
-            square,
-            square,
-            square,
+            pltpu.VMEM(strips, BF16),
+            pltpu.VMEM((width, 2 * STEP), BF16),
             square,
             square,
             pltpu.VMEM(strips, jnp.float32),

time: 40 us -> 39.3 us (0.982)
  Pallas kernels: 37.4 us -> 36.8 us
    pallas_call x1, Pallas kernels: 37.4 us -> 36.8 us  [shards(): pl.pallas_call(functools.partial(kernel, sectors), out_shape=jax.ShapeDty...]
where the time goes in v3:
time: 39.3 us; the launch traced here: 39.1 us
  Pallas kernels  36.8 us (94%)
  local copies, waits for them, and re-layouts  2.36 us (6%)
    pallas_call x1, Pallas kernels, shards(): pl.pallas_call(functools.partial(kernel, sectors), out_shape=jax.ShapeDty...  36.8 us
    unnamed x1, local copies, waits for them, and re-layouts  2.36 us

profile of v3, /device:TPU:13, one launch (start us, length us, event | category | flops | bytes accessed | tf_op | source)
XLA Modules:
  0.0 39.1 jit_solution(11453614882252336669)
XLA Ops:
  0.0 36.8 %shard_map.55 = bf16[1,1,768,768]{3,2,1,0:T(8,128)(2,1)} custom-call(f32[2,4,4]{2,1,0:T(4,128)} %coupling_hbm.1, s32[8]{0:T(128)} %sec_size_hbm.1, bf16[1,1,768,768]{3,2,1,0:T(8,128)(2,1)} %psi_hbm.1, bf16[2,1,768,768]{3,2,1,0:T(8,128)(2,1)} %left_hbm.1, bf16[2,1,768,768]{3,2,1,0:T(8,128)(2,1)} %right_hbm.1), custom_call_target="tpu_custom_call" | custom-call | tf_op jit(solution)/shard_map/pallas_call | solution.py:392
  36.8 2.4 %copy.7 = bf16[1,1,768,768]{3,2,1,0:T(8,128)(2,1)} copy(bf16[1,1,768,768]{3,2,1,0:T(8,128)(2,1)} %shard_map.55) | data formatting | bytes 2359296

commit v4 on v3

--- a/solution.py
+++ b/solution.py
@@ -59,7 +59,7 @@
 ):
     width = own.shape[0]
     steps = width // STEP
-    early = steps // 2
+    early = steps - 1
     p = lax.axis_index("panel")
     pair = lax.axis_index("chan")
     last = sectors - 1

time: 39.3 us -> 40.4 us (1.028)
  Pallas kernels: 36.8 us -> 37.7 us
    pallas_call x1, Pallas kernels: 36.8 us -> 37.7 us  [shards(): pl.pallas_call(functools.partial(kernel, sectors), out_shape=jax.ShapeDty...]
where the time goes in v4:
time: 40.4 us; the launch traced here: 40.1 us
  Pallas kernels  37.7 us (93%)
  local copies, waits for them, and re-layouts  2.36 us (6%)
    pallas_call x1, Pallas kernels, shards(): pl.pallas_call(functools.partial(kernel, sectors), out_shape=jax.ShapeDty...  37.7 us
    unnamed x1, local copies, waits for them, and re-layouts  2.36 us

profile of v4, /device:TPU:13, one launch (start us, length us, event | category | flops | bytes accessed | tf_op | source)
XLA Modules:
  0.0 40.1 jit_solution(8110891020296165245)
XLA Ops:
  0.0 37.7 %shard_map.55 = bf16[1,1,768,768]{3,2,1,0:T(8,128)(2,1)} custom-call(f32[2,4,4]{2,1,0:T(4,128)} %coupling_hbm.1, s32[8]{0:T(128)} %sec_size_hbm.1, bf16[1,1,768,768]{3,2,1,0:T(8,128)(2,1)} %psi_hbm.1, bf16[2,1,768,768]{3,2,1,0:T(8,128)(2,1)} %left_hbm.1, bf16[2,1,768,768]{3,2,1,0:T(8,128)(2,1)} %right_hbm.1), custom_call_target="tpu_custom_call" | custom-call | tf_op jit(solution)/shard_map/pallas_call | solution.py:392
  37.7 2.4 %copy.7 = bf16[1,1,768,768]{3,2,1,0:T(8,128)(2,1)} copy(bf16[1,1,768,768]{3,2,1,0:T(8,128)(2,1)} %shard_map.55) | data formatting | bytes 2359296
